TPU v7x, 128 devices: a whole 4x4x4 slice. The times are simulated.
128 devices in a mesh: side: 2 (over y_hi), tok: 4 (over x), vocab: 16 (over y_lo, z, core).
Axes of the slice: x: 4, y: 4 (y_hi: 2, y_lo: 2; y = y_hi * 2 + y_lo), z: 4, core: 2. Of those that a mesh axis runs over, the one named last changes fastest.
Arguments:
- teacher_hidden: bfloat16 [1024, 5120], P('tok', 'side'), may hold values from -48 to 48
- teacher_head: bfloat16 [5120, 38912], P('side', 'vocab'), may hold values from -1 to 1
- student_hidden: bfloat16 [1024, 4096], P('tok', 'side'), may hold values from -48 to 48
- student_head: bfloat16 [4096, 38912], P('side', 'vocab'), may hold values from -1 to 1
- sampled_ids: int32 [1024], P('tok'), may hold values from 0 to 38911
Outputs:
- token_kl: float32 [1024], P('tok')
- sampled_gap: float32 [1024], P('tok')
- hidden_grad: bfloat16 [1024, 4096], P('tok', ('side', 'vocab'))
- head_grad: float32 [4096, 38912], P(('side', 'tok'), 'vocab')
All inputs are finite; a program needn't handle non-finite values.
Results may differ from a plain program's by a relative error of at most 0.009.
Values may be sent and summed in bfloat16 or wider, within the bound.
A program may use at most 128 MiB of HBM per device.

v0:
```python
import jax
import jax.numpy as jnp
from jax import lax
from jax.sharding import PartitionSpec as P


def body(teacher_hidden, teacher_head, student_hidden, student_head, sampled_ids):
    teacher_part = jnp.dot(teacher_hidden, teacher_head, preferred_element_type=jnp.float32)
    student_part = jnp.dot(student_hidden, student_head, preferred_element_type=jnp.float32)
    teacher_logits, student_logits = (
        lax.psum_scatter(teacher_part, "side", scatter_dimension=1, tiled=True),
        lax.psum_scatter(student_part, "side", scatter_dimension=1, tiled=True),
    )
    share_width = teacher_logits.shape[1]
    shard_width = teacher_head.shape[1]
    first_column = lax.axis_index("vocab") * shard_width + lax.axis_index("side") * share_width
    columns = first_column + jnp.arange(share_width, dtype=jnp.int32)
    matches = columns[None, :] == sampled_ids[:, None]
    difference = student_logits - teacher_logits
    peak_teacher, peak_student = lax.pmax(
        (jnp.max(teacher_logits, axis=1), jnp.max(student_logits, axis=1)), ("side", "vocab")
    )
    student_exp = jnp.exp(student_logits - peak_student[:, None])
    total_teacher, total_student, weighted, picked = lax.psum(
        (
            jnp.sum(jnp.exp(teacher_logits - peak_teacher[:, None]), axis=1),
            jnp.sum(student_exp, axis=1),
            jnp.sum(student_exp * difference, axis=1),
            jnp.sum(jnp.where(matches, difference, 0.0), axis=1),
        ),
        ("side", "vocab"),
    )
    norm_teacher = peak_teacher + jnp.log(total_teacher)
    norm_student = peak_student + jnp.log(total_student)
    token_kl = weighted / total_student - norm_student + norm_teacher
    sampled_gap = picked - norm_student + norm_teacher
    student_logp = student_logits - norm_student[:, None]
    teacher_logp = teacher_logits - norm_teacher[:, None]
    probs = jnp.exp(student_logp)
    grad_share = (probs * (student_logp - teacher_logp - token_kl[:, None])).astype(jnp.bfloat16)
    logit_grad = lax.all_gather(grad_share, "side", axis=1, tiled=True)
    hidden_grad = lax.psum_scatter(
        lax.dot_general(
            student_head, logit_grad, (((1,), (1,)), ((), ())), preferred_element_type=jnp.float32
        ),
        "vocab",
        scatter_dimension=0,
        tiled=True,
    ).T.astype(jnp.bfloat16)
    token_count = student_hidden.shape[0] * lax.axis_size("tok")
    head_grad = (
        lax.psum_scatter(
            lax.dot_general(
                student_hidden,
                logit_grad,
                (((0,), (0,)), ((), ())),
                preferred_element_type=jnp.float32,
            ),
            "tok",
            scatter_dimension=0,
            tiled=True,
        )
        / token_count
    )
    return (token_kl, sampled_gap, hidden_grad, head_grad)


def solution(mesh):
    placed = (P("tok", "side"), P("side", "vocab"), P("tok", "side"), P("side", "vocab"), P("tok"))
    return jax.shard_map(
        body,
        mesh=mesh,
        in_specs=placed,
        out_specs=(P("tok"), P("tok"), P("tok", ("side", "vocab")), P(("side", "tok"), "vocab")),
        check_vma=False,
    )
```

profile of v0, /device:TPU:1, one launch (start us, length us, event | category | flops | bytes accessed | tf_op | source)
XLA Modules:
  0.0 523.7 jit_solution(4687888877489272049)
XLA Ops:
  7.2 0.0 reduce-scatter.7.cloned.1.call-start
  7.2 1.3 copy-done
  8.5 9.3 %fusion.2 = f32[256,2432]{0,1:T(8,128)} fusion(bf16[256,2560]{1,0:T(8,128)(2,1)S(1)} %copy-done, bf16[2560,2432]{1,0:T(8,128)(2,1)} %param.6), kind=kOutput, calls=%fused_computation.16 | convolution fusion | flops 3187671040 | bytes 16252928 | tf_op jit(solution)/shard_map/dot_general | solution.py:8
  17.8 0.0 reduce-scatter.7.cloned.1.call-update
  17.9 0.0 reduce-scatter.5.cloned.1.call-start
  17.9 1.1 copy-done.5
  19.1 9.3 %fusion.1 = f32[256,2432]{0,1:T(8,128)} fusion(bf16[256,2048]{1,0:T(8,128)(2,1)S(1)} %copy-done.5, bf16[2048,2432]{1,0:T(8,128)(2,1)} %param.8), kind=kOutput, calls=%fused_computation.15 | convolution fusion | flops 2550136832 | bytes 13500416 | tf_op jit(solution)/shard_map/dot_general | solution.py:9
  28.3 0.0 reduce-scatter.5.cloned.1.call-update
  28.3 0.0 all-gather.2.cloned.1.call-start
  28.4 33.0 %reduce-scatter.7.cloned.1.call-done = f32[256,1216]{0,1:T(8,128)} async-done(((f32[256,2432]{0,1:T(8,128)}), f32[256,1216]{0,1:T(8,128)}) %reduce-scatter.7.cloned.1.call-update) | async-done | bytes 1245200 | tf_op jit(solution)/shard_map/reduce_scatter | solution.py:11
  61.4 1.6 reduce_max.19
  63.0 41.1 %reduce-scatter.5.cloned.1.call-done = f32[256,1216]{0,1:T(8,128)} async-done(((f32[256,2432]{0,1:T(8,128)}), f32[256,1216]{0,1:T(8,128)}) %reduce-scatter.5.cloned.1.call-update) | async-done | bytes 1245200 | tf_op jit(solution)/shard_map/reduce_scatter | solution.py:12
  104.1 1.6 reduce_max.18
  105.6 62.7 %all-reduce.1 = (f32[256]{0:T(256)S(1)}, f32[256]{0:T(256)S(1)}) all-reduce(f32[256]{0:T(256)S(1)} %reduce_max.19, f32[256]{0:T(256)S(1)} %reduce_max.18), channel_id=1, replica_groups=mesh['side'=2,'tok'=4,'vocab'=16] {'side','vocab'}, use_global_device_ids=true, to_apply=%region_9.10 | all-reduce | flops 512 | bytes 4096 | tf_op jit(solution)/shard_map/pmax | solution.py:20
  168.4 0.6 select_reduce_fusion
  169.0 65.6 %all-reduce = (f32[256]{0:T(256)S(1)}, f32[256]{0:T(256)S(1)}, f32[256]{0:T(256)S(1)}, f32[256]{0:T(256)S(1)}) all-reduce(f32[256]{0:T(256)S(1)} %get-tuple-element.11, f32[256]{0:T(256)S(1)} %get-tuple-element.10, f32[256]{0:T(256)S(1)} %get-tuple-element.9, ...), channel_id=1, replica_groups=mesh['side'=2,'tok'=4,'vocab'=16] {'side','vocab'}, use_global_device_ids=true, to_apply=%region_11.12 | all-reduce | flops 1024 | bytes 8192 | tf_op jit(solution)/shard_map/psum | solution.py:24
  234.6 0.6 subtract_add_fusion
  235.2 1.1 multiply_convert_fusion
  236.3 0.0 all-gather.2.cloned.1.call-update
  236.3 0.0 reduce-scatter.9.cloned.1.call-start
  236.4 23.9 %all-gather.2.cloned.1.call-done = bf16[256,2432]{0,1:T(8,128)(2,1)} async-done(((bf16[256,1216]{0,1:T(8,128)(2,1)}), bf16[256,2432]{0,1:T(8,128)(2,1)}) %all-gather.2.cloned.1.call-update) | async-done | bytes 1245200 | tf_op jit(solution)/shard_map/all_gather | solution.py:41
  260.3 8.5 %convolution_bitcast_fusion.1 = f32[2048,256]{0,1:T(8,128)} fusion(bf16[256,2432]{0,1:T(8,128)(2,1)} %all-gather.2.cloned.1.call-done, bf16[2048,2432]{1,0:T(8,128)(2,1)} %param.8), kind=kOutput, calls=%fused_computation.1 | convolution fusion | flops 2550136832 | bytes 13303808 | tf_op jit(solution)/shard_map/dot_general | solution.py:43
  268.8 0.0 reduce-scatter.9.cloned.1.call-update
  268.8 0.2 reduce-scatter.11.cloned.1.call-start
  269.1 1.0 copy-done.4
  270.1 8.3 %convolution_bitcast_fusion = f32[2048,2432]{0,1:T(8,128)} fusion(bf16[256,2432]{0,1:T(8,128)(2,1)S(1)} %copy-done.4, bf16[256,2048]{1,0:T(8,128)(2,1)S(1)} %copy-done.6), kind=kOutput, calls=%fused_computation | convolution fusion | flops 2550136832 | bytes 22216704 | tf_op jit(solution)/shard_map/dot_general | solution.py:53
  278.4 0.0 reduce-scatter.11.cloned.1.call-update
  278.5 49.6 %reduce-scatter.9.cloned.1.call-done = f32[128,256]{0,1:T(8,128)} async-done(((f32[2048,256]{0,1:T(8,128)}), f32[128,256]{0,1:T(8,128)}) %reduce-scatter.9.cloned.1.call-update) | async-done | bytes 131088 | tf_op jit(solution)/shard_map/reduce_scatter | solution.py:42
  328.1 1.5 convert_bitcast_fusion
  329.6 176.4 %reduce-scatter.11.cloned.1.call-done = f32[512,2432]{0,1:T(8,128)} async-done(((f32[2048,2432]{0,1:T(8,128)}), f32[512,2432]{0,1:T(8,128)}) %reduce-scatter.11.cloned.1.call-update) | async-done | bytes 4980752 | tf_op jit(solution)/shard_map/reduce_scatter | solution.py:52
  506.1 5.2 broadcast_multiply_fusion
  511.3 5.8 %copy.9 = f32[512,2432]{1,0:T(8,128)} copy(f32[512,2432]{0,1:T(8,128)} %broadcast_multiply_fusion) | data formatting | bytes 9961472
  (17 shorter events, 0.0 us)
Async XLA Ops:
  7.2 1.3 copy-start
  7.2 54.2 %reduce-scatter.7.cloned.1.call-start = ((), (), s32[]{:S(2)}) async-start(), calls=%async_computation.5 | async-start | bytes 3735552 | tf_op jit(solution)/shard_map/reduce_scatter | solution.py:11
  17.8 1.2 copy-start.5
  17.9 86.2 %reduce-scatter.5.cloned.1.call-start = ((), (), s32[]{:S(2)}) async-start(), calls=%async_computation.4 | async-start | bytes 3735552 | tf_op jit(solution)/shard_map/reduce_scatter | solution.py:12
  28.3 231.9 %all-gather.2.cloned.1.call-start = ((), (), s32[]{:S(2)}) async-start(), calls=%async_computation.6 | async-start | bytes 1867776 | tf_op jit(solution)/shard_map/all_gather | solution.py:41
  28.4 140.0 %copy-start.8 = (s32[256]{0:T(256)S(1)}, s32[256]{0:T(256)}, u32[]{:S(2)}) copy-start(s32[256]{0:T(256)} %param.9) | copy-start | bytes 3076
  61.4 107.0 %copy-start.2 = (f32[256,1216]{0,1:T(8,128)S(1)}, f32[256,1216]{0,1:T(8,128)}, u32[]{:S(2)}) copy-start(f32[256,1216]{0,1:T(8,128)} %reduce-scatter.7.cloned.1.call-done) | copy-start | bytes 3735556
  104.1 64.3 %copy-start.3 = (f32[256,1216]{0,1:T(8,128)S(1)}, f32[256,1216]{0,1:T(8,128)}, u32[]{:S(2)}) copy-start(f32[256,1216]{0,1:T(8,128)} %reduce-scatter.5.cloned.1.call-done) | copy-start | bytes 3735556
  235.2 1.1 copy-start.7
  236.3 91.8 %reduce-scatter.9.cloned.1.call-start = ((), (), s32[]{:S(2)}) async-start(), calls=%async_computation.7 | async-start | bytes 2228224 | tf_op jit(solution)/shard_map/reduce_scatter | solution.py:42
  260.3 8.8 %copy-start.6 = (bf16[256,2048]{1,0:T(8,128)(2,1)S(1)}, bf16[256,2048]{1,0:T(8,128)(2,1)}, u32[]{:S(2)}) copy-start(bf16[256,2048]{1,0:T(8,128)(2,1)} %param.7) | copy-start | bytes 3145732
  268.8 1.3 copy-start.4
  268.8 237.2 %reduce-scatter.11.cloned.1.call-start = ((), (), s32[]{:S(2)}) async-start(), calls=%async_computation.8 | async-start | bytes 24903680 | tf_op jit(solution)/shard_map/reduce_scatter | solution.py:52
  511.3 5.9 %copy-start.1 = (bf16[256,2560]{1,0:T(8,128)(2,1)S(1)}, bf16[256,2560]{1,0:T(8,128)(2,1)}, u32[]{:S(2)}) copy-start(bf16[256,2560]{1,0:T(8,128)(2,1)} %param.5) | copy-start | bytes 3932164
Sparse Core Ops, SparseCore 0:
  18.0 43.3 reduce-scatter.6
  64.5 39.5 reduce-scatter.4
  236.5 23.7 all-gather.1
  269.0 59.0 reduce-scatter.8
  330.4 175.5 reduce-scatter.10
where the time goes:
time: 524 us
  waiting for transfers between devices  324 us (62%)
  blocking collectives  128 us (24%)
  matrix products  35.5 us (7%)
  between operations  13.8 us (3%)
  other arithmetic  12.2 us (2%)
  local copies, waits for them, and re-layouts  9.32 us (2%)
    reduce_scatter x1, waiting for transfers between devices, body(): lax.psum_scatter(lax.dot_general(student_hidden, logit_grad, (((0,), (0,)...  176 us
    psum x1, blocking collectives, body(): lax.psum((jnp.sum(jnp.exp(teacher_logits - peak_teacher[:, None]), axis=1...  65.6 us
    pmax x1, blocking collectives, body(): lax.pmax((jnp.max(teacher_logits, axis=1), jnp.max(student_logits, axis=1...  62.7 us
    reduce_scatter x1, waiting for transfers between devices, body(): lax.psum_scatter(lax.dot_general(student_head, logit_grad, (((1,), (1,)),...  49.6 us
    reduce_scatter x1, waiting for transfers between devices, body(): lax.psum_scatter(student_part, 'side', scatter_dimension=1, tiled=True)  41.1 us
    reduce_scatter x1, waiting for transfers between devices, body(): lax.psum_scatter(teacher_part, 'side', scatter_dimension=1, tiled=True)  33 us
    all_gather x1, waiting for transfers between devices, body(): logit_grad = lax.all_gather(grad_share, 'side', axis=1, tiled=True)  23.9 us
  transfers between devices with their start and end apart: 5, of which 5 were waited for; matrix products, arithmetic and copies ran while one was open for 4% of the time, Pallas kernels for 0%

commit v1 on v0

v1 whole, which is shorter than its diff:
```python
import functools

import jax
import jax.numpy as jnp
from jax import lax
from jax.experimental import pallas as pl
from jax.experimental.pallas import tpu as pltpu
from jax.sharding import PartitionSpec as P

MESH = pl.DeviceIdType.MESH
F32, BF16 = jnp.float32, jnp.bfloat16
CHUNKS = 4
LANES = 128
GROUP = 8
MIB = 1024 * 1024


def tiles(width, step):
    return [(at, min(step, width - at)) for at in range(0, width, step)]


def fold(parts):
    peak_s = functools.reduce(jnp.maximum, [p[0:1] for p in parts])
    peak_t = functools.reduce(jnp.maximum, [p[3:4] for p in parts])
    sum_s = weighted = sum_t = picked = jnp.zeros_like(peak_s)
    for p in parts:
        scale = jnp.exp(p[0:1] - peak_s)
        sum_s += p[1:2] * scale
        weighted += p[2:3] * scale
        sum_t += p[4:5] * jnp.exp(p[3:4] - peak_t)
        picked += p[5:6]
    return peak_s, sum_s, weighted, peak_t, sum_t, picked


def stack(rows):
    sub = lax.broadcasted_iota(jnp.int32, (8, LANES), 0)
    out = jnp.zeros((8, LANES), F32)
    for k, row in enumerate(rows):
        out = jnp.where(sub == k, row, out)
    return out


def main_kernel(
    th, sh, ids, thead, shead,
    g_out, ht_out, hid_out, kl_out, gap_out,
    wt, ws, pt, ps, rt, rs, gbuf, hall, ht,
    st_own, st_core, st_mid, st_grp, hg, hc, h2s, h2r, res, res_in,
    ls_sem, lt_sem, p_send, p_recv, cs_send, cs_recv, gs_send, gs_recv,
    y_send, y_recv, x_send, x_recv, l_sem, hx_send, hx_recv, hl_sem,
    hc_send, hc_recv, h2_send, h2_recv, r_send, r_recv,
):
    side, tok, voc = lax.axis_index("side"), lax.axis_index("tok"), lax.axis_index("vocab")
    core, grp = lax.rem(voc, 2), voc // 2
    side_peer = (1 - side, tok, voc)
    core_peer = (side, tok, voc + 1 - 2 * core)

    def x_at(k):
        return lax.rem(tok + k, 4)

    def x_peer(k):
        return (side, x_at(k), voc)

    def grp_at(k):
        return lax.rem(grp + k, GROUP)

    def grp_peer(k):
        return (side, tok, grp_at(k) * 2 + core)

    tokens, depth_s = sh.shape
    half = tokens // 2
    rows = half // CHUNKS
    width = ws.shape[1]
    feats = depth_s // 4
    blocks = width // LANES
    own0 = pl.multiple_of(side * half, half)
    far0 = pl.multiple_of((1 - side) * half, half)

    def remote(src, dst, send, recv, peer):
        return pltpu.make_async_remote_copy(
            src_ref=src, dst_ref=dst, send_sem=send, recv_sem=recv, device_id=peer, device_id_type=MESH
        )

    step = 256
    spans = tiles(width, step)

    def load(j, head, w, sem):
        at, n = spans[j]
        return pltpu.make_async_copy(head.at[:, pl.ds(at, n)], w.at[:, pl.ds(at, n)], sem.at[j])

    for j in range(len(spans)):
        load(j, shead, ws, ls_sem).start()
    for j in range(len(spans)):
        load(j, thead, wt, lt_sem).start()

    barrier = pltpu.get_barrier_semaphore()
    peers = [side_peer, core_peer] + [x_peer(k) for k in (1, 2, 3)] + [grp_peer(k) for k in range(1, GROUP)]
    for peer in peers:
        pl.semaphore_signal(barrier, inc=1, device_id=peer, device_id_type=MESH)
    pl.semaphore_wait(barrier, len(peers))

    def hidden_copy(k):
        return remote(
            sh.at[:, pl.ds(pl.multiple_of(x_at(k) * feats, feats), feats)],
            hall.at[tok],
            hx_send.at[k - 1],
            hx_recv.at[k - 1],
            x_peer(k),
        )

    for k in (1, 2, 3):
        hidden_copy(k).start()
    hidden_own = pltpu.make_async_copy(
        sh.at[:, pl.ds(pl.multiple_of(tok * feats, feats), feats)], hall.at[tok], hl_sem.at[0]
    )
    hidden_own.start()

    def matmul(h, head, w, sem, p):
        for j, (at, n) in enumerate(spans):
            load(j, head, w, sem).wait()
            p[:, at : at + n] = jnp.dot(h[...], w[:, at : at + n], preferred_element_type=F32)

    def partial_copy(model, c):
        src, dst = ((ps, rs), (pt, rt))[model]
        return remote(
            src.at[pl.ds(pl.multiple_of(far0 + c * rows, rows), rows), :],
            dst.at[pl.ds(c * rows, rows), :],
            p_send.at[model, c],
            p_recv.at[model, c],
            side_peer,
        )

    matmul(sh, shead, ws, ls_sem, ps)
    partial_copy(0, 0).start()
    matmul(th, thead, wt, lt_sem, pt)
    partial_copy(1, 0).start()
    partial_copy(0, 1).start()
    partial_copy(1, 1).start()

    hidden_own.wait()
    for k in (1, 2, 3):
        hidden_copy(k).wait()
    for k in range(4):
        ht[:, k * tokens : (k + 1) * tokens] = hall[k].T
    ht_copy = pltpu.make_async_copy(ht, ht_out, hl_sem.at[1])
    ht_copy.start()

    lane = lax.broadcasted_iota(jnp.int32, (rows, LANES), 1)
    sub = lax.broadcasted_iota(jnp.int32, (rows, LANES), 0)
    lane_row = lax.broadcasted_iota(jnp.int32, (1, LANES), 1)
    id_row = jnp.where(side == 0, ids[0:1, :], ids[1:2, :]).astype(F32)
    first = voc * width

    def core_stats(c):
        return remote(st_own.at[c], st_core.at[c], cs_send.at[c], cs_recv.at[c], core_peer)

    def grp_stats(c, k):
        return remote(st_mid.at[c], st_grp.at[c, grp], gs_send.at[c, k - 1], gs_recv.at[c, k - 1], grp_peer(k))

    def side_grad(c):
        return remote(gbuf.at[c, 0], gbuf.at[c, 1], y_send.at[c], y_recv.at[c], side_peer)

    def grad_rows(c, which):
        begin = tok * tokens + (own0 if which == 0 else far0) + c * rows
        return g_out.at[pl.ds(pl.multiple_of(begin, rows), rows), :]

    def x_grad(c, which, k):
        return remote(
            gbuf.at[c, which], grad_rows(c, which), x_send.at[c, which, k - 1], x_recv.at[c, which, k - 1], x_peer(k)
        )

    def local_grad(c, which):
        return pltpu.make_async_copy(gbuf.at[c, which], grad_rows(c, which), l_sem.at[c, which])

    def hidden_core(c):
        return remote(hg.at[c, 1 - core], hc.at[c], hc_send.at[c], hc_recv.at[c], core_peer)

    def hidden_grp(c, k):
        return remote(
            h2s.at[c, grp_at(k)], h2r.at[c, grp], h2_send.at[c, k - 1], h2_recv.at[c, k - 1], grp_peer(k)
        )

    def hidden_matmul(c, begin, end):
        g = gbuf[c].reshape(2 * rows, width)

        @pl.loop(begin, end)
        def _(f):
            w = ws[pl.ds(pl.multiple_of(f * 2 * LANES, 2 * LANES), 2 * LANES), :]
            r = lax.dot_general(g, w, (((1,), (1,)), ((), ())), preferred_element_type=F32).astype(BF16)
            hg[c, 0, f] = r[:, :LANES]
            hg[c, 1, f] = r[:, LANES:]

    def hidden_second(c):
        hidden_core(c).wait()
        h2s[c] = (hg[c, core].astype(F32) + hc[c].astype(F32)).astype(BF16)
        for k in range(1, GROUP):
            hidden_grp(c, k).start()

    def hidden_final(c):
        for k in range(1, GROUP):
            hidden_grp(c, k).wait()
        total = h2s[c, grp].astype(F32)
        for k in range(1, GROUP):
            total += h2r[c, grp_at(k)].astype(F32)
        total = total.astype(BF16)
        hid_out[pl.ds(pl.multiple_of(own0 + c * rows, rows), rows), :] = total[:rows]
        hid_out[pl.ds(pl.multiple_of(far0 + c * rows, rows), rows), :] = total[rows:]

    for c in range(CHUNKS):
        mine = pl.ds(pl.multiple_of(own0 + c * rows, rows), rows)
        theirs = pl.ds(c * rows, rows)
        eye = lane == sub + c * rows

        def to_row(col):
            return jnp.sum(jnp.where(eye, col, 0.0), axis=0, keepdims=True)

        def to_col(row):
            return jnp.sum(jnp.where(eye, row, 0.0), axis=1, keepdims=True)

        partial_copy(0, c).wait()
        partial_copy(1, c).wait()
        if c + 2 < CHUNKS:
            partial_copy(0, c + 2).start()
            partial_copy(1, c + 2).start()

        top_s = top_t = jnp.full((rows, LANES), -jnp.inf, F32)
        for j in range(blocks):
            cols = slice(j * LANES, (j + 1) * LANES)
            s = ps[mine, cols] + rs[theirs, cols]
            t = pt[mine, cols] + rt[theirs, cols]
            ps[mine, cols] = s
            pt[mine, cols] = t
            top_s, top_t = jnp.maximum(top_s, s), jnp.maximum(top_t, t)
        top_s = jnp.max(top_s, axis=1, keepdims=True)
        top_t = jnp.max(top_t, axis=1, keepdims=True)
        target = to_col(id_row).astype(jnp.int32) - first
        sum_s = weighted = sum_t = picked = jnp.zeros((rows, LANES), F32)
        for j in range(blocks):
            cols = slice(j * LANES, (j + 1) * LANES)
            s, t = ps[mine, cols], pt[mine, cols]
            e, d = jnp.exp(s - top_s), s - t
            sum_s += e
            weighted += e * d
            sum_t += jnp.exp(t - top_t)
            picked += jnp.where(lane + j * LANES == target, d, 0.0)
        sums = [jnp.sum(a, axis=1, keepdims=True) for a in (sum_s, weighted, sum_t, picked)]
        st_own[c] = stack([to_row(a) for a in (top_s, sums[0], sums[1], top_t, sums[2], sums[3])])
        core_stats(c).start()

        if c > 0:
            hidden_matmul(c - 1, 0, 2)

        core_stats(c).wait()
        st_mid[c] = stack(fold([st_own[c], st_core[c]]))
        for k in range(1, GROUP):
            grp_stats(c, k).start()

        if c > 0:
            hidden_matmul(c - 1, 2, 4)

        for k in range(1, GROUP):
            grp_stats(c, k).wait()
        parts = [st_mid[c]] + [st_grp[c, grp_at(k)] for k in range(1, GROUP)]
        peak_s, sum_s, weighted, peak_t, sum_t, picked = fold(parts)
        norm_s = peak_s + jnp.log(sum_s)
        norm_t = peak_t + jnp.log(sum_t)
        mean = weighted / sum_s
        here = (lane_row >= c * rows) & (lane_row < (c + 1) * rows)
        kl = jnp.where(here, mean - norm_s + norm_t, 0.0 if c == 0 else res[0:1])
        gap = jnp.where(here, picked - norm_s + norm_t, 0.0 if c == 0 else res[1:2])
        res[...] = stack([kl, gap])
        norm_col, mean_col = to_col(norm_s), to_col(mean)
        for j in range(blocks):
            cols = slice(j * LANES, (j + 1) * LANES)
            s, t = ps[mine, cols], pt[mine, cols]
            gbuf[c, 0, :, cols] = (jnp.exp(s - norm_col) * (s - t - mean_col)).astype(BF16)
        side_grad(c).start()
        for k in (1, 3, 2):
            x_grad(c, 0, k).start()
        local_grad(c, 0).start()

        if c > 0:
            hidden_matmul(c - 1, 4, GROUP)
            hidden_core(c - 1).start()

        side_grad(c).wait()
        for k in (1, 3, 2):
            x_grad(c, 1, k).start()
        local_grad(c, 1).start()
        if c > 0:
            hidden_second(c - 1)

    last = CHUNKS - 1
    row_copy = remote(res, res_in, r_send.at[0], r_recv.at[0], side_peer)
    row_copy.start()
    hidden_matmul(last, 0, GROUP)
    hidden_core(last).start()
    hidden_second(last)
    row_copy.wait()
    kl_out[0:1] = jnp.where(side == 0, res[0:1], res_in[0:1])
    kl_out[1:2] = jnp.where(side == 0, res_in[0:1], res[0:1])
    gap_out[0:1] = jnp.where(side == 0, res[1:2], res_in[1:2])
    gap_out[1:2] = jnp.where(side == 0, res_in[1:2], res[1:2])
    for c in range(CHUNKS):
        hidden_final(c)
    ht_copy.wait()
    for c in range(CHUNKS):
        for which in (0, 1):
            local_grad(c, which).wait()
            for k in (1, 2, 3):
                x_grad(c, which, k).wait()


def last_kernel(scale, ht, g, hid, kl, gap, out, hid_out, kl_out, gap_out):
    out[...] = jnp.dot(ht[...], g[...], preferred_element_type=F32) * scale

    @pl.when(pl.program_id(0) == 0)
    def _():
        hid_out[...] = hid[...]
        kl_out[...] = kl[...]
        gap_out[...] = gap[...]


def body(teacher_hidden, teacher_head, student_hidden, student_head, sampled_ids):
    tokens, depth_s = student_hidden.shape
    depth_t, width = teacher_head.shape
    toks = lax.axis_size("tok")
    half = tokens // 2
    rows = half // CHUNKS
    feats = depth_s // toks
    loads = len(tiles(width, 256))
    vmem, anywhere = pl.BlockSpec(memory_space=pltpu.VMEM), pl.BlockSpec(memory_space=pl.ANY)
    dma = pltpu.SemaphoreType.DMA
    g, ht, hid, kl, gap = pl.pallas_call(
        main_kernel,
        name="exchange",
        out_shape=(
            jax.ShapeDtypeStruct((toks * tokens, width), BF16),
            jax.ShapeDtypeStruct((feats, toks * tokens), BF16),
            jax.ShapeDtypeStruct((tokens, LANES), BF16),
            jax.ShapeDtypeStruct((2, LANES), F32),
            jax.ShapeDtypeStruct((2, LANES), F32),
        ),
        in_specs=[vmem, vmem, vmem, anywhere, anywhere],
        out_specs=(anywhere, anywhere, vmem, vmem, vmem),
        scratch_shapes=[
            pltpu.VMEM((depth_t, width), BF16),
            pltpu.VMEM((depth_s, width), BF16),
            pltpu.VMEM((tokens, width), F32),
            pltpu.VMEM((tokens, width), F32),
            pltpu.VMEM((half, width), F32),
            pltpu.VMEM((half, width), F32),
            pltpu.VMEM((CHUNKS, 2, rows, width), BF16),
            pltpu.VMEM((toks, tokens, feats), BF16),
            pltpu.VMEM((feats, toks * tokens), BF16),
            pltpu.VMEM((CHUNKS, 8, LANES), F32),
            pltpu.VMEM((CHUNKS, 8, LANES), F32),
            pltpu.VMEM((CHUNKS, 8, LANES), F32),
            pltpu.VMEM((CHUNKS, GROUP, 8, LANES), F32),
            pltpu.VMEM((CHUNKS, 2, GROUP, 2 * rows, LANES), BF16),
            pltpu.VMEM((CHUNKS, GROUP, 2 * rows, LANES), BF16),
            pltpu.VMEM((CHUNKS, GROUP, 2 * rows, LANES), BF16),
            pltpu.VMEM((CHUNKS, GROUP, 2 * rows, LANES), BF16),
            pltpu.VMEM((8, LANES), F32),
            pltpu.VMEM((8, LANES), F32),
            dma((loads,)),
            dma((loads,)),
            dma((2, CHUNKS)),
            dma((2, CHUNKS)),
            dma((CHUNKS,)),
            dma((CHUNKS,)),
            dma((CHUNKS, GROUP - 1)),
            dma((CHUNKS, GROUP - 1)),
            dma((CHUNKS,)),
            dma((CHUNKS,)),
            dma((CHUNKS, 2, 3)),
            dma((CHUNKS, 2, 3)),
            dma((CHUNKS, 2)),
            dma((3,)),
            dma((3,)),
            dma((2,)),
            dma((CHUNKS,)),
            dma((CHUNKS,)),
            dma((CHUNKS, GROUP - 1)),
            dma((CHUNKS, GROUP - 1)),
            dma((1,)),
            dma((1,)),
        ],
        compiler_params=pltpu.CompilerParams(
            collective_id=0, has_side_effects=True, vmem_limit_bytes=60 * MIB
        ),
    )(teacher_hidden, student_hidden, sampled_ids.reshape(2, LANES), teacher_head, student_head)

    step = 512
    whole = lambda a: pl.BlockSpec(a.shape, lambda j: (0,) * a.ndim)
    head_grad, hid, kl, gap = pl.pallas_call(
        functools.partial(last_kernel, 1.0 / (toks * tokens)),
        name="head_grad",
        grid=(pl.cdiv(width, step),),
        out_shape=(
            jax.ShapeDtypeStruct((feats, width), F32),
            jax.ShapeDtypeStruct(hid.shape, hid.dtype),
            jax.ShapeDtypeStruct(kl.shape, kl.dtype),
            jax.ShapeDtypeStruct(gap.shape, gap.dtype),
        ),
        in_specs=[whole(ht), pl.BlockSpec((toks * tokens, step), lambda j: (0, j)), whole(hid), whole(kl), whole(gap)],
        out_specs=(pl.BlockSpec((feats, step), lambda j: (0, j)), whole(hid), whole(kl), whole(gap)),
        compiler_params=pltpu.CompilerParams(vmem_limit_bytes=40 * MIB),
    )(ht, g, hid, kl, gap)
    return (kl.reshape(tokens), gap.reshape(tokens), hid, head_grad)


def solution(mesh):
    placed = (P("tok", "side"), P("side", "vocab"), P("tok", "side"), P("side", "vocab"), P("tok"))
    return jax.shard_map(
        body,
        mesh=mesh,
        in_specs=placed,
        out_specs=(P("tok"), P("tok"), P("tok", ("side", "vocab")), P(("side", "tok"), "vocab")),
        check_vma=False,
    )
```

time: 524 us -> 135 us (0.26)
  waiting for transfers between devices: 324 us -> 0 us
  Pallas kernels: 0 us -> 128 us
  blocking collectives: 128 us -> 0 us
  matrix products: 35.5 us -> 0 us
  between operations: 13.8 us -> 0.65 us
  other arithmetic: 12.2 us -> 0 us
    reduce_scatter x4 -> x0, waiting for transfers between devices: 300 us -> none  [the longest x1 176 us: body(): lax.psum_scatter(lax.dot_general(student_hidden, logit_grad, (((0,), (0,)...]
    pallas_call x0 -> x2, Pallas kernels: none -> 128 us  [the longest x1 123 us: body(): pl.pallas_call(main_kernel, name='exchange', out_shape=(jax.ShapeDtypeStr...]
    psum x1 -> x0, blocking collectives: 65.6 us -> none  [body(): lax.psum((jnp.sum(jnp.exp(teacher_logits - peak_teacher[:, None]), axis=1...]
    pmax x1 -> x0, blocking collectives: 62.7 us -> none  [body(): lax.pmax((jnp.max(teacher_logits, axis=1), jnp.max(student_logits, axis=1...]
    dot_general x4 -> x0, matrix products: 35.5 us -> none  [the longest x1 9.34 us: body(): jnp.dot(teacher_hidden, teacher_head, preferred_element_type=jnp.float32)]
    all_gather x1 -> x0, waiting for transfers between devices: 23.9 us -> none  [body(): logit_grad = lax.all_gather(grad_share, 'side', axis=1, tiled=True)]
  transfers between devices with their start and end apart: 5 -> 0, of which waited for: 5 -> 0; matrix products, arithmetic and copies ran while one was open for 4% -> 0% of each run, Pallas kernels for 0% -> 0%
where the time goes in v1:
time: 135 us
  Pallas kernels  128 us (95%)
  local copies, waits for them, and re-layouts  5.76 us (4%)
    pallas_call x1, Pallas kernels, body(): pl.pallas_call(main_kernel, name='exchange', out_shape=(jax.ShapeDtypeStr...  123 us
    unnamed x10, local copies, waits for them, and re-layouts  5.76 us
    pallas_call x1, Pallas kernels, body(): pl.pallas_call(functools.partial(last_kernel, 1.0 / (toks * tokens)), nam...  5.23 us

profile of v1, /device:TPU:1, one launch (start us, length us, event | category | flops | bytes accessed | tf_op | source)
XLA Modules:
  0.0 134.7 jit_solution(10355239234684552840)
XLA Ops:
  0.6 123.1 %exchange.1 = (bf16[1024,2432]{1,0:T(8,128)(2,1)}, bf16[512,1024]{1,0:T(8,128)(2,1)}, bf16[256,128]{1,0:T(8,128)(2,1)}, f32[2,128]{1,0:T(2,128)}, f32[2,128]{1,0:T(2,128)}) custom-call(bf16[256,2560]{1,0:T(8,128)(2,1)} %th.1, bf16[256,2048]{1,0:T(8,128)(2,1)} %sh.1, s32[2,128]{1,0:T(2,128)} %bitcast.3, bf16[2560,2432]{1,0:T(8,128)(2,1)} %thead.1, ...), custom_call_target="tpu_custom_call" | custom-call | tf_op jit(solution)/shard_map/exchange/pallas_call | solution.py:333
  123.7 0.0 copy-start
  123.7 2.4 %copy-done = bf16[1024,2432]{1,0:T(8,128)(2,1)S(1)} copy-done((bf16[1024,2432]{1,0:T(8,128)(2,1)S(1)}, bf16[1024,2432]{1,0:T(8,128)(2,1)}, u32[]{:S(2)}) %copy-start) | copy-done | bytes 4980760
  126.1 0.0 copy-start.1
  126.1 1.2 copy-done.1
  127.3 0.0 copy-start.2
  127.3 0.8 copy-done.2
  128.2 0.0 copy-start.3
  128.2 0.7 copy-done.3
  128.8 0.0 copy-start.4
  128.8 0.6 copy-done.4
  129.5 5.2 %head_grad.1 = (f32[512,2432]{1,0:T(8,128)}, bf16[256,128]{1,0:T(8,128)(2,1)}, f32[2,128]{1,0:T(2,128)}, f32[2,128]{1,0:T(2,128)}) custom-call(bf16[512,1024]{1,0:T(8,128)(2,1)S(1)} %copy-done.1, bf16[1024,2432]{1,0:T(8,128)(2,1)S(1)} %copy-done, bf16[256,128]{1,0:T(8,128)(2,1)S(1)} %copy-done.2, f32[2,128]{1,0:T(2,128)S(1)} %copy-done.3, f32[2,128]{1,0:T(2,128)S(1)} %copy-done.4), custom_call_target="tpu_custom_call" | custom-call | tf_op jit(solution)/shard_map/head_grad/pallas_call | solution.py:395
Async XLA Ops:
  123.7 2.4 %copy-start = (bf16[1024,2432]{1,0:T(8,128)(2,1)S(1)}, bf16[1024,2432]{1,0:T(8,128)(2,1)}, u32[]{:S(2)}) copy-start(bf16[1024,2432]{1,0:T(8,128)(2,1)} %get-tuple-element.14.g) | copy-start | bytes 14942212
  126.1 1.2 copy-start.1
  127.3 0.8 copy-start.2
  128.2 0.7 copy-start.3
  128.8 0.6 copy-start.4

commit v2 on v1

v2 whole, which is shorter than its diff:
```python
import functools

import jax
import jax.numpy as jnp
from jax import lax
from jax.experimental import pallas as pl
from jax.experimental.pallas import tpu as pltpu
from jax.sharding import PartitionSpec as P

MESH = pl.DeviceIdType.MESH
F32, BF16 = jnp.float32, jnp.bfloat16
CHUNKS = 8
PAIRS = CHUNKS // 2
LANES = 128
GROUP = 8
BITS = 21
TOP = float(2 ** (BITS - 1) - 1)
BIAS = 2 ** (BITS - 1)
MASK = 2**BITS - 1
LOW = 32 - BITS
LOAD = 512
MIB = 1024 * 1024
MAIN_VMEM, LAST_VMEM = 42, 16


def tiles(width, step):
    return [(at, min(step, width - at)) for at in range(0, width, step)]


def fold(parts):
    peak_s = functools.reduce(jnp.maximum, [p[0:1] for p in parts])
    peak_t = functools.reduce(jnp.maximum, [p[3:4] for p in parts])
    sum_s = weighted = sum_t = picked = jnp.zeros_like(peak_s)
    for p in parts:
        scale = jnp.exp(p[0:1] - peak_s)
        sum_s += p[1:2] * scale
        weighted += p[2:3] * scale
        sum_t += p[4:5] * jnp.exp(p[3:4] - peak_t)
        picked += p[5:6]
    return peak_s, sum_s, weighted, peak_t, sum_t, picked


def stack(rows):
    sub = lax.broadcasted_iota(jnp.int32, (8, LANES), 0)
    out = jnp.zeros((8, LANES), F32)
    for k, row in enumerate(rows):
        out = jnp.where(sub == k, row, out)
    return out


def encode(u, v, w):
    return u | (w << BITS), v | ((w >> LOW) << BITS)


def decode(a, b):
    high = lax.shift_right_logical(a, BITS) | (lax.shift_right_logical(b, BITS) << LOW)
    return a & MASK, b & MASK, high


def words(blocks):
    return 2 * (blocks // 3) + blocks % 3


def main_kernel(
    th_in, sh_in, ids, thead, shead,
    g_out, ht_out, hid_out, kl_out, gap_out,
    th, sh, wt, ws, pt, ps, wt_out, ws_out, wt_in, ws_in, gbuf, hall, ht,
    sc_out, sc_in, st_own, st_core, st_mid, st_grp, hg, hc, h2s, h2r, res, res_in,
    in_sem, ls_sem, lt_sem, sc_send, sc_recv, p_send, p_recv, cs_send, cs_recv, gs_send, gs_recv,
    y_send, y_recv, x_send, x_recv, l_sem, hx_send, hx_recv, hl_sem,
    hc_send, hc_recv, h2_send, h2_recv, r_send, r_recv,
):
    side, tok, voc = lax.axis_index("side"), lax.axis_index("tok"), lax.axis_index("vocab")
    core, grp = lax.rem(voc, 2), voc // 2
    side_peer = (1 - side, tok, voc)
    core_peer = (side, tok, voc + 1 - 2 * core)

    def x_at(k):
        return lax.rem(tok + k, 4)

    def x_peer(k):
        return (side, x_at(k), voc)

    def grp_at(k):
        return lax.rem(grp + k, GROUP)

    def grp_peer(k):
        return (side, tok, grp_at(k) * 2 + core)

    tokens, depth_s = sh.shape
    half = tokens // 2
    rows = half // CHUNKS
    pair_rows = 2 * rows
    width = ws.shape[1]
    feats = depth_s // 4
    blocks = width // LANES
    own0 = pl.multiple_of(side * half, half)
    far0 = pl.multiple_of((1 - side) * half, half)
    own, far = pl.ds(own0, half), pl.ds(far0, half)

    def remote(src, dst, send, recv, peer):
        return pltpu.make_async_remote_copy(
            src_ref=src, dst_ref=dst, send_sem=send, recv_sem=recv, device_id=peer, device_id_type=MESH
        )

    spans = tiles(width, LOAD)

    def load(j, head, w, sem):
        at, n = spans[j]
        return pltpu.make_async_copy(head.at[:, pl.ds(at, n)], w.at[:, pl.ds(at, n)], sem.at[j])

    sh_copy = pltpu.make_async_copy(sh_in, sh, in_sem.at[0])
    th_copy = pltpu.make_async_copy(th_in, th, in_sem.at[1])
    sh_copy.start()
    for j in range(len(spans)):
        load(j, shead, ws, ls_sem).start()
    th_copy.start()
    for j in range(len(spans)):
        load(j, thead, wt, lt_sem).start()

    barrier = pltpu.get_barrier_semaphore()
    peers = [side_peer, core_peer] + [x_peer(k) for k in (1, 2, 3)] + [grp_peer(k) for k in range(1, GROUP)]
    for peer in peers:
        pl.semaphore_signal(barrier, inc=1, device_id=peer, device_id_type=MESH)
    pl.semaphore_wait(barrier, len(peers))

    def hidden_copy(k):
        return remote(
            sh.at[:, pl.ds(pl.multiple_of(x_at(k) * feats, feats), feats)],
            hall.at[tok],
            hx_send.at[k - 1],
            hx_recv.at[k - 1],
            x_peer(k),
        )

    hidden_own = pltpu.make_async_copy(
        sh.at[:, pl.ds(pl.multiple_of(tok * feats, feats), feats)], hall.at[tok], hl_sem.at[0]
    )
    ht_copy = pltpu.make_async_copy(ht, ht_out, hl_sem.at[1])
    sh_copy.wait()
    for k in (1, 2, 3):
        hidden_copy(k).start()
    hidden_own.start()

    def transpose_hidden():
        hidden_own.wait()
        for k in (1, 2, 3):
            hidden_copy(k).wait()
        for k in range(4):
            ht[:, k * tokens : (k + 1) * tokens] = hall[k].T
        ht_copy.start()

    def matmul(h, head, w, sem, p):
        for j, (at, n) in enumerate(spans):
            load(j, head, w, sem).wait()
            p[:, at : at + n] = jnp.dot(h[...], w[:, at : at + n], preferred_element_type=F32)

    def scale_copy(model):
        return remote(sc_out.at[model], sc_in.at[model], sc_send.at[model], sc_recv.at[model], side_peer)

    def partial_copy(model, c):
        src, dst = ((ws_out, ws_in), (wt_out, wt_in))[model]
        at = pl.ds(c * rows, rows)
        return remote(src.at[at, :], dst.at[at, :], p_send.at[model, c], p_recv.at[model, c], side_peer)

    def code(model):
        p, out = ((ps, ws_out), (pt, wt_out))[model]
        top = jnp.zeros((half, LANES), F32)
        for j in range(blocks):
            top = jnp.maximum(top, jnp.abs(p[far, j * LANES : (j + 1) * LANES]))
        top = jnp.maximum(jnp.max(top, axis=1, keepdims=True), 1e-30)
        eye = lax.broadcasted_iota(jnp.int32, (half, LANES), 0) == lax.broadcasted_iota(jnp.int32, (half, LANES), 1)
        sc_out[model] = stack([jnp.sum(jnp.where(eye, top * (1.0 / TOP), 0.0), axis=0, keepdims=True)])
        scale_copy(model).start()
        inverse = TOP / top

        def codes(j):
            return (p[far, j * LANES : (j + 1) * LANES] * inverse + (BIAS + 0.5)).astype(jnp.int32)

        for k in range(blocks // 3):
            a, b = encode(codes(3 * k), codes(3 * k + 1), codes(3 * k + 2))
            out[:, 2 * k * LANES : (2 * k + 1) * LANES] = a
            out[:, (2 * k + 1) * LANES : (2 * k + 2) * LANES] = b
        for k in range(blocks % 3):
            at = (blocks // 3 * 2 + k) * LANES
            out[:, at : at + LANES] = codes(blocks // 3 * 3 + k)

    matmul(sh, shead, ws, ls_sem, ps)
    code(0)
    partial_copy(0, 0).start()
    partial_copy(0, 1).start()
    th_copy.wait()
    matmul(th, thead, wt, lt_sem, pt)
    code(1)
    partial_copy(1, 0).start()
    partial_copy(1, 1).start()

    lane = lax.broadcasted_iota(jnp.int32, (rows, LANES), 1)
    sub = lax.broadcasted_iota(jnp.int32, (rows, LANES), 0)
    lane_row = lax.broadcasted_iota(jnp.int32, (1, LANES), 1)
    id_row = jnp.where(side == 0, ids[0:1, :], ids[1:2, :]).astype(F32)
    first = voc * width

    def to_row(col, c):
        return jnp.sum(jnp.where(lane == sub + c * rows, col, 0.0), axis=0, keepdims=True)

    def to_col(row, c):
        return jnp.sum(jnp.where(lane == sub + c * rows, row, 0.0), axis=1, keepdims=True)

    def core_stats(c):
        return remote(st_own.at[c], st_core.at[c], cs_send.at[c], cs_recv.at[c], core_peer)

    def grp_stats(c, k):
        return remote(st_mid.at[c], st_grp.at[c, grp], gs_send.at[c, k - 1], gs_recv.at[c, k - 1], grp_peer(k))

    def grad_part(c, which):
        return gbuf.at[c // 2, which, pl.ds(c % 2 * rows, rows), :]

    def grad_rows(c, which):
        begin = tok * tokens + (own0 if which == 0 else far0) + c * rows
        return g_out.at[pl.ds(pl.multiple_of(begin, rows), rows), :]

    def side_grad(c):
        return remote(grad_part(c, 0), grad_part(c, 1), y_send.at[c], y_recv.at[c], side_peer)

    def x_grad(c, which, k):
        return remote(
            grad_part(c, which),
            grad_rows(c, which),
            x_send.at[c, which, k - 1],
            x_recv.at[c, which, k - 1],
            x_peer(k),
        )

    def local_grad(c, which):
        return pltpu.make_async_copy(grad_part(c, which), grad_rows(c, which), l_sem.at[c, which])

    def hidden_core(p):
        return remote(hg.at[p, 1 - core], hc.at[p], hc_send.at[p], hc_recv.at[p], core_peer)

    def hidden_grp(p, k):
        return remote(
            h2s.at[p, grp_at(k)], h2r.at[p, grp], h2_send.at[p, k - 1], h2_recv.at[p, k - 1], grp_peer(k)
        )

    def hidden_matmul(p, begin, end):
        g = gbuf[p].reshape(2 * pair_rows, width)

        @pl.loop(begin, end)
        def _(f):
            w = ws[pl.ds(pl.multiple_of(f * 2 * LANES, 2 * LANES), 2 * LANES), :]
            r = lax.dot_general(g, w, (((1,), (1,)), ((), ())), preferred_element_type=F32).astype(BF16)
            hg[p, 0, f] = r[:, :LANES]
            hg[p, 1, f] = r[:, LANES:]

    def hidden_second(p):
        hidden_core(p).wait()
        h2s[p] = (hg[p, core].astype(F32) + hc[p].astype(F32)).astype(BF16)
        for k in range(1, GROUP):
            hidden_grp(p, k).start()

    def hidden_final(p):
        for k in range(1, GROUP):
            hidden_grp(p, k).wait()
        total = h2s[p, grp].astype(F32)
        for k in range(1, GROUP):
            total += h2r[p, grp_at(k)].astype(F32)
        total = total.astype(BF16)
        hid_out[pl.ds(pl.multiple_of(own0 + p * pair_rows, pair_rows), pair_rows), :] = total[:pair_rows]
        hid_out[pl.ds(pl.multiple_of(far0 + p * pair_rows, pair_rows), pair_rows), :] = total[pair_rows:]

    def mine(c):
        return pl.ds(pl.multiple_of(own0 + c * rows, rows), rows)

    def sums_and_stats(c):
        tops = []
        for model, (p, w) in enumerate(((ps, ws_in), (pt, wt_in))):
            if c == 0:
                scale_copy(model).wait()
            partial_copy(model, c).wait()
            scale = to_col(sc_in[model, 0:1, :], c)
            top = jnp.full((rows, LANES), -jnp.inf, F32)
            theirs = pl.ds(c * rows, rows)

            def word(k):
                return w[theirs, k * LANES : (k + 1) * LANES]

            for k in range(blocks // 3):
                for n, u in enumerate(decode(word(2 * k), word(2 * k + 1))):
                    cols = slice((3 * k + n) * LANES, (3 * k + n + 1) * LANES)
                    v = p[mine(c), cols] + (u - BIAS).astype(F32) * scale
                    p[mine(c), cols] = v
                    top = jnp.maximum(top, v)
            for k in range(blocks % 3):
                at = (blocks // 3 * 3 + k) * LANES
                v = p[mine(c), at : at + LANES] + (word(blocks // 3 * 2 + k) - BIAS).astype(F32) * scale
                p[mine(c), at : at + LANES] = v
                top = jnp.maximum(top, v)
            tops.append(jnp.max(top, axis=1, keepdims=True))
        top_s, top_t = tops
        target = to_col(id_row, c).astype(jnp.int32) - first
        sum_s = weighted = sum_t = picked = jnp.zeros((rows, LANES), F32)
        for j in range(blocks):
            cols = slice(j * LANES, (j + 1) * LANES)
            s, t = ps[mine(c), cols], pt[mine(c), cols]
            e, d = jnp.exp(s - top_s), s - t
            sum_s += e
            weighted += e * d
            sum_t += jnp.exp(t - top_t)
            picked += jnp.where(lane + j * LANES == target, d, 0.0)
        sums = [jnp.sum(a, axis=1, keepdims=True) for a in (sum_s, weighted, sum_t, picked)]
        st_own[c] = stack([to_row(a, c) for a in (top_s, sums[0], sums[1], top_t, sums[2], sums[3])])
        core_stats(c).start()

    def join_core(c):
        core_stats(c).wait()
        st_mid[c] = stack(fold([st_own[c], st_core[c]]))
        for k in range(1, GROUP):
            grp_stats(c, k).start()

    def grads(c):
        for k in range(1, GROUP):
            grp_stats(c, k).wait()
        parts = [st_mid[c]] + [st_grp[c, grp_at(k)] for k in range(1, GROUP)]
        peak_s, sum_s, weighted, peak_t, sum_t, picked = fold(parts)
        norm_s = peak_s + jnp.log(sum_s)
        norm_t = peak_t + jnp.log(sum_t)
        mean = weighted / sum_s
        here = (lane_row >= c * rows) & (lane_row < (c + 1) * rows)
        kl = jnp.where(here, mean - norm_s + norm_t, 0.0 if c == 0 else res[0:1])
        gap = jnp.where(here, picked - norm_s + norm_t, 0.0 if c == 0 else res[1:2])
        res[...] = stack([kl, gap])
        norm_col, mean_col = to_col(norm_s, c), to_col(mean, c)
        for j in range(blocks):
            cols = slice(j * LANES, (j + 1) * LANES)
            s, t = ps[mine(c), cols], pt[mine(c), cols]
            v = (jnp.exp(s - norm_col) * (s - t - mean_col)).astype(BF16)
            gbuf[c // 2, 0, pl.ds(c % 2 * rows, rows), cols] = v
        side_grad(c).start()
        for k in (1, 3, 2):
            x_grad(c, 0, k).start()
        local_grad(c, 0).start()

    def forward(c):
        side_grad(c).wait()
        for k in (1, 3, 2):
            x_grad(c, 1, k).start()
        local_grad(c, 1).start()

    row_copy = remote(res, res_in, r_send.at[0], r_recv.at[0], side_peer)
    for i in range(CHUNKS + 2):
        if i < CHUNKS:
            sums_and_stats(i)
        if 1 <= i <= CHUNKS:
            grads(i - 1)
        if i == CHUNKS:
            row_copy.start()
        if i < CHUNKS:
            join_core(i)
        if i >= 2:
            forward(i - 2)
        if i + 2 < CHUNKS:
            partial_copy(0, i + 2).start()
            partial_copy(1, i + 2).start()
        if i == 1:
            transpose_hidden()
        if i >= 3 and i % 2 == 1:
            p = (i - 3) // 2
            if p > 0:
                hidden_second(p - 1)
            if i < CHUNKS + 1:
                hidden_matmul(p, 0, GROUP // 2)
        if i >= 4 and i % 2 == 0:
            p = (i - 4) // 2
            hidden_matmul(p, GROUP // 2, GROUP)
            hidden_core(p).start()

    last = PAIRS - 1
    hidden_matmul(last, 0, GROUP)
    hidden_core(last).start()
    row_copy.wait()
    kl_out[0:1] = jnp.where(side == 0, res[0:1], res_in[0:1])
    kl_out[1:2] = jnp.where(side == 0, res_in[0:1], res[0:1])
    gap_out[0:1] = jnp.where(side == 0, res[1:2], res_in[1:2])
    gap_out[1:2] = jnp.where(side == 0, res_in[1:2], res[1:2])
    for p in range(last):
        hidden_final(p)
    hidden_second(last)
    hidden_final(last)
    ht_copy.wait()
    for c in range(CHUNKS):
        for which in (0, 1):
            local_grad(c, which).wait()
            for k in (1, 2, 3):
                x_grad(c, which, k).wait()


def last_kernel(scale, ht, g, hid, kl, gap, out, hid_out, kl_out, gap_out):
    out[...] = jnp.dot(ht[...], g[...], preferred_element_type=F32) * scale

    @pl.when(pl.program_id(0) == 0)
    def _():
        hid_out[...] = hid[...]
        kl_out[...] = kl[...]
        gap_out[...] = gap[...]


def body(teacher_hidden, teacher_head, student_hidden, student_head, sampled_ids):
    tokens, depth_s = student_hidden.shape
    depth_t, width = teacher_head.shape
    toks = lax.axis_size("tok")
    half = tokens // 2
    feats = depth_s // toks
    pair_rows = half // PAIRS
    loads = len(tiles(width, LOAD))
    packed = words(width // LANES) * LANES
    vmem, anywhere = pl.BlockSpec(memory_space=pltpu.VMEM), pl.BlockSpec(memory_space=pl.ANY)
    dma = pltpu.SemaphoreType.DMA
    g, ht, hid, kl, gap = pl.pallas_call(
        main_kernel,
        name="exchange",
        out_shape=(
            jax.ShapeDtypeStruct((toks * tokens, width), BF16),
            jax.ShapeDtypeStruct((feats, toks * tokens), BF16),
            jax.ShapeDtypeStruct((tokens, LANES), BF16),
            jax.ShapeDtypeStruct((2, LANES), F32),
            jax.ShapeDtypeStruct((2, LANES), F32),
        ),
        in_specs=[anywhere, anywhere, vmem, anywhere, anywhere],
        out_specs=(anywhere, anywhere, vmem, vmem, vmem),
        scratch_shapes=[
            pltpu.VMEM((tokens, depth_t), BF16),
            pltpu.VMEM((tokens, depth_s), BF16),
            pltpu.VMEM((depth_t, width), BF16),
            pltpu.VMEM((depth_s, width), BF16),
            pltpu.VMEM((tokens, width), F32),
            pltpu.VMEM((tokens, width), F32),
            pltpu.VMEM((half, packed), jnp.int32),
            pltpu.VMEM((half, packed), jnp.int32),
            pltpu.VMEM((half, packed), jnp.int32),
            pltpu.VMEM((half, packed), jnp.int32),
            pltpu.VMEM((PAIRS, 2, pair_rows, width), BF16),
            pltpu.VMEM((toks, tokens, feats), BF16),
            pltpu.VMEM((feats, toks * tokens), BF16),
            pltpu.VMEM((2, 8, LANES), F32),
            pltpu.VMEM((2, 8, LANES), F32),
            pltpu.VMEM((CHUNKS, 8, LANES), F32),
            pltpu.VMEM((CHUNKS, 8, LANES), F32),
            pltpu.VMEM((CHUNKS, 8, LANES), F32),
            pltpu.VMEM((CHUNKS, GROUP, 8, LANES), F32),
            pltpu.VMEM((PAIRS, 2, GROUP, 2 * pair_rows, LANES), BF16),
            pltpu.VMEM((PAIRS, GROUP, 2 * pair_rows, LANES), BF16),
            pltpu.VMEM((PAIRS, GROUP, 2 * pair_rows, LANES), BF16),
            pltpu.VMEM((PAIRS, GROUP, 2 * pair_rows, LANES), BF16),
            pltpu.VMEM((8, LANES), F32),
            pltpu.VMEM((8, LANES), F32),
            dma((2,)),
            dma((loads,)),
            dma((loads,)),
            dma((2,)),
            dma((2,)),
            dma((2, CHUNKS)),
            dma((2, CHUNKS)),
            dma((CHUNKS,)),
            dma((CHUNKS,)),
            dma((CHUNKS, GROUP - 1)),
            dma((CHUNKS, GROUP - 1)),
            dma((CHUNKS,)),
            dma((CHUNKS,)),
            dma((CHUNKS, 2, 3)),
            dma((CHUNKS, 2, 3)),
            dma((CHUNKS, 2)),
            dma((3,)),
            dma((3,)),
            dma((2,)),
            dma((PAIRS,)),
            dma((PAIRS,)),
            dma((PAIRS, GROUP - 1)),
            dma((PAIRS, GROUP - 1)),
            dma((1,)),
            dma((1,)),
        ],
        compiler_params=pltpu.CompilerParams(
            collective_id=0, has_side_effects=True, vmem_limit_bytes=MAIN_VMEM * MIB
        ),
    )(teacher_hidden, student_hidden, sampled_ids.reshape(2, LANES), teacher_head, student_head)

    step = 512
    whole = lambda a: pl.BlockSpec(a.shape, lambda j: (0,) * a.ndim)
    head_grad, hid, kl, gap = pl.pallas_call(
        functools.partial(last_kernel, 1.0 / (toks * tokens)),
        name="head_grad",
        grid=(pl.cdiv(width, step),),
        out_shape=(
            jax.ShapeDtypeStruct((feats, width), F32),
            jax.ShapeDtypeStruct(hid.shape, hid.dtype),
            jax.ShapeDtypeStruct(kl.shape, kl.dtype),
            jax.ShapeDtypeStruct(gap.shape, gap.dtype),
        ),
        in_specs=[whole(ht), pl.BlockSpec((toks * tokens, step), lambda j: (0, j)), whole(hid), whole(kl), whole(gap)],
        out_specs=(pl.BlockSpec((feats, step), lambda j: (0, j)), whole(hid), whole(kl), whole(gap)),
        compiler_params=pltpu.CompilerParams(vmem_limit_bytes=LAST_VMEM * MIB),
    )(ht, g, hid, kl, gap)
    return (kl.reshape(tokens), gap.reshape(tokens), hid, head_grad)


def solution(mesh):
    placed = (P("tok", "side"), P("side", "vocab"), P("tok", "side"), P("side", "vocab"), P("tok"))
    return jax.shard_map(
        body,
        mesh=mesh,
        in_specs=placed,
        out_specs=(P("tok"), P("tok"), P("tok", ("side", "vocab")), P(("side", "tok"), "vocab")),
        check_vma=False,
    )
```

time: 135 us -> 99.1 us (0.73)
  Pallas kernels: 128 us -> 95.1 us
  local copies, waits for them, and re-layouts: 5.76 us -> 3.21 us
    pallas_call x1, Pallas kernels: 123 us -> 89.8 us  [body(): pl.pallas_call(main_kernel, name='exchange', out_shape=(jax.ShapeDtypeStr...]
    unnamed x10 -> x6, local copies, waits for them, and re-layouts: 5.76 us -> 3.21 us
where the time goes in v2:
time: 99.1 us; the launch traced here: 98.9 us
  Pallas kernels  95.1 us (96%)
  local copies, waits for them, and re-layouts  3.21 us (3%)
    pallas_call x1, Pallas kernels, body(): pl.pallas_call(main_kernel, name='exchange', out_shape=(jax.ShapeDtypeStr...  89.8 us
    pallas_call x1, Pallas kernels, body(): pl.pallas_call(functools.partial(last_kernel, 1.0 / (toks * tokens)), nam...  5.28 us
    unnamed x6, local copies, waits for them, and re-layouts  3.21 us

profile of v2, /device:TPU:1, one launch (start us, length us, event | category | flops | bytes accessed | tf_op | source)
XLA Modules:
  0.0 98.9 jit_solution(4057721361836771625)
XLA Ops:
  0.6 0.0 copy-start
  0.6 1.3 %copy-done = bf16[256,2560]{1,0:T(8,128)(2,1)S(1)} copy-done((bf16[256,2560]{1,0:T(8,128)(2,1)S(1)}, bf16[256,2560]{1,0:T(8,128)(2,1)}, u32[]{:S(2)}) %copy-start) | copy-done | bytes 1310744
  1.9 0.0 copy-start.1
  2.0 1.2 %copy-done.1 = bf16[256,2048]{1,0:T(8,128)(2,1)S(1)} copy-done((bf16[256,2048]{1,0:T(8,128)(2,1)S(1)}, bf16[256,2048]{1,0:T(8,128)(2,1)}, u32[]{:S(2)}) %copy-start.1) | copy-done | bytes 1048600
  3.2 0.0 copy-start.2
  3.2 0.7 copy-done.2
  3.9 89.8 %exchange.1 = (bf16[1024,2432]{1,0:T(8,128)(2,1)S(1)}, bf16[512,1024]{1,0:T(8,128)(2,1)S(1)}, bf16[256,128]{1,0:T(8,128)(2,1)S(1)}, f32[2,128]{1,0:T(2,128)S(1)}, f32[2,128]{1,0:T(2,128)S(1)}) custom-call(bf16[256,2560]{1,0:T(8,128)(2,1)S(1)} %copy-done, bf16[256,2048]{1,0:T(8,128)(2,1)S(1)} %copy-done.1, s32[2,128]{1,0:T(2,128)S(1)} %bitcast.3, ...), custom_call_target="tpu_custom_call" | custom-call | tf_op jit(solution)/shard_map/exchange/pallas_call | solution.py:419
  93.7 5.3 %head_grad.1 = (f32[512,2432]{1,0:T(8,128)}, bf16[256,128]{1,0:T(8,128)(2,1)}, f32[2,128]{1,0:T(2,128)}, f32[2,128]{1,0:T(2,128)}) custom-call(bf16[512,1024]{1,0:T(8,128)(2,1)S(1)} %get-tuple-element.13.ht, bf16[1024,2432]{1,0:T(8,128)(2,1)S(1)} %get-tuple-element.14.g, bf16[256,128]{1,0:T(8,128)(2,1)S(1)} %get-tuple-element.15.hid, ...), custom_call_target="tpu_custom_call" | custom-call | tf_op jit(solution)/shard_map/head_grad/pallas_call | solution.py:490
Async XLA Ops:
  0.6 1.3 %copy-start = (bf16[256,2560]{1,0:T(8,128)(2,1)S(1)}, bf16[256,2560]{1,0:T(8,128)(2,1)}, u32[]{:S(2)}) copy-start(bf16[256,2560]{1,0:T(8,128)(2,1)} %th_in.1) | copy-start | bytes 3932164
  1.9 1.2 %copy-start.1 = (bf16[256,2048]{1,0:T(8,128)(2,1)S(1)}, bf16[256,2048]{1,0:T(8,128)(2,1)}, u32[]{:S(2)}) copy-start(bf16[256,2048]{1,0:T(8,128)(2,1)} %sh_in.1) | copy-start | bytes 3145732
  3.2 0.7 copy-start.2

commit v3 on v2

--- a/solution.py
+++ b/solution.py
@@ -10,7 +10,9 @@
 MESH = pl.DeviceIdType.MESH
 F32, BF16 = jnp.float32, jnp.bfloat16
 CHUNKS = 8
-PAIRS = CHUNKS // 2
+PAIRS = 2
+PER = CHUNKS // PAIRS
+AHEAD = 2
 LANES = 128
 GROUP = 8
 BITS = 21
@@ -18,13 +20,23 @@
 BIAS = 2 ** (BITS - 1)
 MASK = 2**BITS - 1
 LOW = 32 - BITS
-LOAD = 512
+STEP = 512
 MIB = 1024 * 1024
 MAIN_VMEM, LAST_VMEM = 42, 16
 
 
 def tiles(width, step):
     return [(at, min(step, width - at)) for at in range(0, width, step)]
+
+
+def columns(width):
+    blocks = width // LANES
+    first = blocks // 6 * 3
+    out = []
+    for begin, end in ((0, first), (first, blocks)):
+        middle = (begin + end + 1) // 2
+        out += [(begin * LANES, (middle - begin) * LANES), (middle * LANES, (end - middle) * LANES)]
+    return out
 
 
 def fold(parts):
@@ -62,9 +74,9 @@
 
 
 def main_kernel(
-    th_in, sh_in, ids, thead, shead,
+    th_in, sh_in, ids_in, thead, shead,
     g_out, ht_out, hid_out, kl_out, gap_out,
-    th, sh, wt, ws, pt, ps, wt_out, ws_out, wt_in, ws_in, gbuf, hall, ht,
+    ids, th, sh, wt, ws, pt, ps, wt_out, ws_out, wt_in, ws_in, gbuf, hall, ht,
     sc_out, sc_in, st_own, st_core, st_mid, st_grp, hg, hc, h2s, h2r, res, res_in,
     in_sem, ls_sem, lt_sem, sc_send, sc_recv, p_send, p_recv, cs_send, cs_recv, gs_send, gs_recv,
     y_send, y_recv, x_send, x_recv, l_sem, hx_send, hx_recv, hl_sem,
@@ -90,7 +102,7 @@
     tokens, depth_s = sh.shape
     half = tokens // 2
     rows = half // CHUNKS
-    pair_rows = 2 * rows
+    pair_rows = PER * rows
     width = ws.shape[1]
     feats = depth_s // 4
     blocks = width // LANES
@@ -103,7 +115,7 @@
             src_ref=src, dst_ref=dst, send_sem=send, recv_sem=recv, device_id=peer, device_id_type=MESH
         )
 
-    spans = tiles(width, LOAD)
+    spans = columns(width)
 
     def load(j, head, w, sem):
         at, n = spans[j]
@@ -117,12 +129,13 @@
     th_copy.start()
     for j in range(len(spans)):
         load(j, thead, wt, lt_sem).start()
+    ids_copy = pltpu.make_async_copy(ids_in, ids, in_sem.at[2])
+    ids_copy.start()
 
     barrier = pltpu.get_barrier_semaphore()
     peers = [side_peer, core_peer] + [x_peer(k) for k in (1, 2, 3)] + [grp_peer(k) for k in range(1, GROUP)]
     for peer in peers:
         pl.semaphore_signal(barrier, inc=1, device_id=peer, device_id_type=MESH)
-    pl.semaphore_wait(barrier, len(peers))
 
     def hidden_copy(k):
         return remote(
@@ -137,11 +150,6 @@
         sh.at[:, pl.ds(pl.multiple_of(tok * feats, feats), feats)], hall.at[tok], hl_sem.at[0]
     )
     ht_copy = pltpu.make_async_copy(ht, ht_out, hl_sem.at[1])
-    sh_copy.wait()
-    for k in (1, 2, 3):
-        hidden_copy(k).start()
-    hidden_own.start()
-
     def transpose_hidden():
         hidden_own.wait()
         for k in (1, 2, 3):
@@ -150,50 +158,77 @@
             ht[:, k * tokens : (k + 1) * tokens] = hall[k].T
         ht_copy.start()
 
-    def matmul(h, head, w, sem, p):
-        for j, (at, n) in enumerate(spans):
+    def matmul(h, head, w, sem, p, part):
+        middle = len(spans) // 2
+        for j in range(middle) if part == 0 else range(middle, len(spans)):
+            at, n = spans[j]
             load(j, head, w, sem).wait()
             p[:, at : at + n] = jnp.dot(h[...], w[:, at : at + n], preferred_element_type=F32)
 
-    def scale_copy(model):
-        return remote(sc_out.at[model], sc_in.at[model], sc_send.at[model], sc_recv.at[model], side_peer)
+    def scale_copy(k):
+        return remote(sc_out.at[k], sc_in.at[k], sc_send.at[k], sc_recv.at[k], side_peer)
+
+    split = spans[len(spans) // 2][0] // LANES
+    parts = ((0, split, 0, words(split)), (split, blocks - split, words(split), words(blocks - split)))
 
     def partial_copy(model, c):
         src, dst = ((ws_out, ws_in), (wt_out, wt_in))[model]
         at = pl.ds(c * rows, rows)
         return remote(src.at[at, :], dst.at[at, :], p_send.at[model, c], p_recv.at[model, c], side_peer)
 
-    def code(model):
+    def early_copy(model, c, part):
+        src, dst = ((ws_out, ws_in), (wt_out, wt_in))[model]
+        at = pl.ds(c * rows, rows), pl.ds(parts[part][2] * LANES, parts[part][3] * LANES)
+        n = part * CHUNKS + c
+        return remote(src.at[at], dst.at[at], p_send.at[model, n], p_recv.at[model, n], side_peer)
+
+    def code(model, part):
         p, out = ((ps, ws_out), (pt, wt_out))[model]
+        block0, count, word0, _ = parts[part]
         top = jnp.zeros((half, LANES), F32)
-        for j in range(blocks):
+        for j in range(block0, block0 + count):
             top = jnp.maximum(top, jnp.abs(p[far, j * LANES : (j + 1) * LANES]))
         top = jnp.maximum(jnp.max(top, axis=1, keepdims=True), 1e-30)
         eye = lax.broadcasted_iota(jnp.int32, (half, LANES), 0) == lax.broadcasted_iota(jnp.int32, (half, LANES), 1)
-        sc_out[model] = stack([jnp.sum(jnp.where(eye, top * (1.0 / TOP), 0.0), axis=0, keepdims=True)])
-        scale_copy(model).start()
+        sc_out[2 * model + part] = stack(
+            [jnp.sum(jnp.where(eye, top * (1.0 / TOP), 0.0), axis=0, keepdims=True)]
+        )
+        scale_copy(2 * model + part).start()
         inverse = TOP / top
 
         def codes(j):
-            return (p[far, j * LANES : (j + 1) * LANES] * inverse + (BIAS + 0.5)).astype(jnp.int32)
-
-        for k in range(blocks // 3):
+            at = (block0 + j) * LANES
+            return (p[far, at : at + LANES] * inverse + (BIAS + 0.5)).astype(jnp.int32)
+
+        def put(k, word):
+            at = (word0 + k) * LANES
+            out[:, at : at + LANES] = word
+
+        for k in range(count // 3):
             a, b = encode(codes(3 * k), codes(3 * k + 1), codes(3 * k + 2))
-            out[:, 2 * k * LANES : (2 * k + 1) * LANES] = a
-            out[:, (2 * k + 1) * LANES : (2 * k + 2) * LANES] = b
-        for k in range(blocks % 3):
-            at = (blocks // 3 * 2 + k) * LANES
-            out[:, at : at + LANES] = codes(blocks // 3 * 3 + k)
-
-    matmul(sh, shead, ws, ls_sem, ps)
-    code(0)
-    partial_copy(0, 0).start()
-    partial_copy(0, 1).start()
+            put(2 * k, a)
+            put(2 * k + 1, b)
+        for k in range(count % 3):
+            put(count // 3 * 2 + k, codes(count // 3 * 3 + k))
+        for c in range(AHEAD):
+            early_copy(model, c, part).start()
+
+    sh_copy.wait()
+    matmul(sh, shead, ws, ls_sem, ps, 0)
+    pl.semaphore_wait(barrier, len(peers))
+    code(0, 0)
+    matmul(sh, shead, ws, ls_sem, ps, 1)
+    code(0, 1)
+    for k in (1, 3, 2):
+        hidden_copy(k).start()
+    hidden_own.start()
     th_copy.wait()
-    matmul(th, thead, wt, lt_sem, pt)
-    code(1)
-    partial_copy(1, 0).start()
-    partial_copy(1, 1).start()
+    matmul(th, thead, wt, lt_sem, pt, 0)
+    code(1, 0)
+    matmul(th, thead, wt, lt_sem, pt, 1)
+    code(1, 1)
+    partial_copy(0, AHEAD).start()
+    ids_copy.wait()
 
     lane = lax.broadcasted_iota(jnp.int32, (rows, LANES), 1)
     sub = lax.broadcasted_iota(jnp.int32, (rows, LANES), 0)
@@ -214,7 +249,7 @@
         return remote(st_mid.at[c], st_grp.at[c, grp], gs_send.at[c, k - 1], gs_recv.at[c, k - 1], grp_peer(k))
 
     def grad_part(c, which):
-        return gbuf.at[c // 2, which, pl.ds(c % 2 * rows, rows), :]
+        return gbuf.at[c // PER, which, pl.ds(c % PER * rows, rows), :]
 
     def grad_rows(c, which):
         begin = tok * tokens + (own0 if which == 0 else far0) + c * rows
@@ -232,39 +267,58 @@
             x_peer(k),
         )
 
+    def spread(c, which):
+        for k in (1, 3, 2):
+            x_grad(c, which, k).start()
+        local_grad(c, which).start()
+
+    def spread_end(c, which):
+        local_grad(c, which).wait()
+        for k in (1, 2, 3):
+            x_grad(c, which, k).wait()
+
     def local_grad(c, which):
         return pltpu.make_async_copy(grad_part(c, which), grad_rows(c, which), l_sem.at[c, which])
 
-    def hidden_core(p):
-        return remote(hg.at[p, 1 - core], hc.at[p], hc_send.at[p], hc_recv.at[p], core_peer)
+    order = (*range(1, GROUP), 0)
+
+    def hidden_core(p, k):
+        f = grp_at(k)
+        return remote(hg.at[p, 1 - core, f], hc.at[p, f], hc_send.at[p, k], hc_recv.at[p, k], core_peer)
 
     def hidden_grp(p, k):
         return remote(
             h2s.at[p, grp_at(k)], h2r.at[p, grp], h2_send.at[p, k - 1], h2_recv.at[p, k - 1], grp_peer(k)
         )
 
-    def hidden_matmul(p, begin, end):
+    def hidden_first(p, k):
+        f = grp_at(k)
+        w = ws[pl.ds(pl.multiple_of(f * 2 * LANES, 2 * LANES), 2 * LANES), :]
         g = gbuf[p].reshape(2 * pair_rows, width)
-
-        @pl.loop(begin, end)
-        def _(f):
-            w = ws[pl.ds(pl.multiple_of(f * 2 * LANES, 2 * LANES), 2 * LANES), :]
-            r = lax.dot_general(g, w, (((1,), (1,)), ((), ())), preferred_element_type=F32).astype(BF16)
-            hg[p, 0, f] = r[:, :LANES]
-            hg[p, 1, f] = r[:, LANES:]
-
-    def hidden_second(p):
-        hidden_core(p).wait()
-        h2s[p] = (hg[p, core].astype(F32) + hc[p].astype(F32)).astype(BF16)
-        for k in range(1, GROUP):
+        r = lax.dot_general(g, w, (((1,), (1,)), ((), ())), preferred_element_type=F32).astype(BF16)
+        hg[p, 0, f] = r[:, :LANES]
+        hg[p, 1, f] = r[:, LANES:]
+        hidden_core(p, k).start()
+
+    def hidden_second(p, k):
+        f = grp_at(k)
+        hidden_core(p, k).wait()
+        h2s[p, f] = (hg[p, core, f].astype(F32) + hc[p, f].astype(F32)).astype(BF16)
+        if k > 0:
             hidden_grp(p, k).start()
 
+    def hidden_steps(p, begin, end):
+        for n in range(begin, end):
+            if n < GROUP:
+                hidden_first(p, order[n])
+            if 0 <= n - 2 < GROUP:
+                hidden_second(p, order[n - 2])
+
     def hidden_final(p):
+        total = h2s[p, grp].astype(F32)
         for k in range(1, GROUP):
             hidden_grp(p, k).wait()
-        total = h2s[p, grp].astype(F32)
-        for k in range(1, GROUP):
-            total += h2r[p, grp_at(k)].astype(F32)
+            total += h2r[p, grp_at(GROUP - k)].astype(F32)
         total = total.astype(BF16)
         hid_out[pl.ds(pl.multiple_of(own0 + p * pair_rows, pair_rows), pair_rows), :] = total[:pair_rows]
         hid_out[pl.ds(pl.multiple_of(far0 + p * pair_rows, pair_rows), pair_rows), :] = total[pair_rows:]
@@ -276,26 +330,28 @@
         tops = []
         for model, (p, w) in enumerate(((ps, ws_in), (pt, wt_in))):
             if c == 0:
-                scale_copy(model).wait()
-            partial_copy(model, c).wait()
-            scale = to_col(sc_in[model, 0:1, :], c)
+                scale_copy(2 * model).wait()
+                scale_copy(2 * model + 1).wait()
+            if c < AHEAD:
+                early_copy(model, c, 0).wait()
+                early_copy(model, c, 1).wait()
+            else:
+                partial_copy(model, c).wait()
             top = jnp.full((rows, LANES), -jnp.inf, F32)
             theirs = pl.ds(c * rows, rows)
-
-            def word(k):
-                return w[theirs, k * LANES : (k + 1) * LANES]
-
-            for k in range(blocks // 3):
-                for n, u in enumerate(decode(word(2 * k), word(2 * k + 1))):
-                    cols = slice((3 * k + n) * LANES, (3 * k + n + 1) * LANES)
+            for part, (block0, count, word0, _) in enumerate(parts):
+                scale = to_col(sc_in[2 * model + part, 0:1, :], c)
+
+                def word(k):
+                    return w[theirs, (word0 + k) * LANES : (word0 + k + 1) * LANES]
+
+                codes = [u for k in range(count // 3) for u in decode(word(2 * k), word(2 * k + 1))]
+                codes += [word(count // 3 * 2 + k) for k in range(count % 3)]
+                for k, u in enumerate(codes):
+                    cols = slice((block0 + k) * LANES, (block0 + k + 1) * LANES)
                     v = p[mine(c), cols] + (u - BIAS).astype(F32) * scale
                     p[mine(c), cols] = v
                     top = jnp.maximum(top, v)
-            for k in range(blocks % 3):
-                at = (blocks // 3 * 3 + k) * LANES
-                v = p[mine(c), at : at + LANES] + (word(blocks // 3 * 2 + k) - BIAS).astype(F32) * scale
-                p[mine(c), at : at + LANES] = v
-                top = jnp.maximum(top, v)
             tops.append(jnp.max(top, axis=1, keepdims=True))
         top_s, top_t = tops
         target = to_col(id_row, c).astype(jnp.int32) - first
@@ -335,74 +391,70 @@
             cols = slice(j * LANES, (j + 1) * LANES)
             s, t = ps[mine(c), cols], pt[mine(c), cols]
             v = (jnp.exp(s - norm_col) * (s - t - mean_col)).astype(BF16)
-            gbuf[c // 2, 0, pl.ds(c % 2 * rows, rows), cols] = v
+            gbuf[c // PER, 0, pl.ds(c % PER * rows, rows), cols] = v
         side_grad(c).start()
-        for k in (1, 3, 2):
-            x_grad(c, 0, k).start()
-        local_grad(c, 0).start()
+        spread(c, 0)
 
     def forward(c):
         side_grad(c).wait()
-        for k in (1, 3, 2):
-            x_grad(c, 1, k).start()
-        local_grad(c, 1).start()
+        spread(c, 1)
 
     row_copy = remote(res, res_in, r_send.at[0], r_recv.at[0], side_peer)
-    for i in range(CHUNKS + 2):
-        if i < CHUNKS:
-            sums_and_stats(i)
-        if 1 <= i <= CHUNKS:
+    for i in range(CHUNKS):
+        end = i == CHUNKS - 1
+        sums_and_stats(i)
+        if end:
+            join_core(i)
+        if i >= 1:
             grads(i - 1)
-        if i == CHUNKS:
-            row_copy.start()
-        if i < CHUNKS:
+        if not end:
             join_core(i)
-        if i >= 2:
-            forward(i - 2)
+        if AHEAD < i + 2 < CHUNKS:
+            partial_copy(0, i + 2).start()
         if i + 2 < CHUNKS:
-            partial_copy(0, i + 2).start()
             partial_copy(1, i + 2).start()
-        if i == 1:
+        if i == 3:
             transpose_hidden()
-        if i >= 3 and i % 2 == 1:
-            p = (i - 3) // 2
-            if p > 0:
-                hidden_second(p - 1)
-            if i < CHUNKS + 1:
-                hidden_matmul(p, 0, GROUP // 2)
-        if i >= 4 and i % 2 == 0:
-            p = (i - 4) // 2
-            hidden_matmul(p, GROUP // 2, GROUP)
-            hidden_core(p).start()
-
-    last = PAIRS - 1
-    hidden_matmul(last, 0, GROUP)
-    hidden_core(last).start()
+        if i == PER + 1:
+            hidden_steps(0, 0, GROUP // 2)
+        if i == PER + 2:
+            hidden_steps(0, GROUP // 2, GROUP + 2)
+        if i >= 1 and not end:
+            forward(i - 1)
+    grads(CHUNKS - 1)
+    row_copy.start()
+    forward(CHUNKS - 2)
+    hidden_final(0)
+    forward(CHUNKS - 1)
+    hidden_steps(1, 0, GROUP)
     row_copy.wait()
     kl_out[0:1] = jnp.where(side == 0, res[0:1], res_in[0:1])
     kl_out[1:2] = jnp.where(side == 0, res_in[0:1], res[0:1])
     gap_out[0:1] = jnp.where(side == 0, res[1:2], res_in[1:2])
     gap_out[1:2] = jnp.where(side == 0, res_in[1:2], res[1:2])
-    for p in range(last):
-        hidden_final(p)
-    hidden_second(last)
-    hidden_final(last)
+    hidden_steps(1, GROUP, GROUP + 2)
+    hidden_final(1)
     ht_copy.wait()
     for c in range(CHUNKS):
         for which in (0, 1):
-            local_grad(c, which).wait()
-            for k in (1, 2, 3):
-                x_grad(c, which, k).wait()
-
-
-def last_kernel(scale, ht, g, hid, kl, gap, out, hid_out, kl_out, gap_out):
-    out[...] = jnp.dot(ht[...], g[...], preferred_element_type=F32) * scale
-
-    @pl.when(pl.program_id(0) == 0)
-    def _():
-        hid_out[...] = hid[...]
-        kl_out[...] = kl[...]
-        gap_out[...] = gap[...]
+            spread_end(c, which)
+
+
+def last_kernel(scale, ht, g, hid, kl, gap, out, hid_out, kl_out, gap_out, buf, sem):
+    spans = tiles(g.shape[1], STEP)
+
+    def store(j):
+        at, n = spans[j]
+        return pltpu.make_async_copy(buf.at[:, pl.ds(at, n)], out.at[:, pl.ds(at, n)], sem.at[j])
+
+    for j, (at, n) in enumerate(spans):
+        buf[:, at : at + n] = jnp.dot(ht[...], g[:, at : at + n], preferred_element_type=F32) * scale
+        store(j).start()
+    hid_out[...] = hid[...]
+    kl_out[...] = kl[...]
+    gap_out[...] = gap[...]
+    for j in range(len(spans)):
+        store(j).wait()
 
 
 def body(teacher_hidden, teacher_head, student_hidden, student_head, sampled_ids):
@@ -412,9 +464,11 @@
     half = tokens // 2
     feats = depth_s // toks
     pair_rows = half // PAIRS
-    loads = len(tiles(width, LOAD))
-    packed = words(width // LANES) * LANES
+    loads = len(columns(width))
+    middle = columns(width)[loads // 2][0] // LANES
+    packed = (words(middle) + words(width // LANES - middle)) * LANES
     vmem, anywhere = pl.BlockSpec(memory_space=pltpu.VMEM), pl.BlockSpec(memory_space=pl.ANY)
+    hbm = pl.BlockSpec(memory_space=pltpu.HBM)
     dma = pltpu.SemaphoreType.DMA
     g, ht, hid, kl, gap = pl.pallas_call(
         main_kernel,
@@ -426,9 +480,10 @@
             jax.ShapeDtypeStruct((2, LANES), F32),
             jax.ShapeDtypeStruct((2, LANES), F32),
         ),
-        in_specs=[anywhere, anywhere, vmem, anywhere, anywhere],
+        in_specs=[hbm] * 5,
         out_specs=(anywhere, anywhere, vmem, vmem, vmem),
         scratch_shapes=[
+            pltpu.VMEM((2, LANES), jnp.int32),
             pltpu.VMEM((tokens, depth_t), BF16),
             pltpu.VMEM((tokens, depth_s), BF16),
             pltpu.VMEM((depth_t, width), BF16),
@@ -442,8 +497,8 @@
             pltpu.VMEM((PAIRS, 2, pair_rows, width), BF16),
             pltpu.VMEM((toks, tokens, feats), BF16),
             pltpu.VMEM((feats, toks * tokens), BF16),
-            pltpu.VMEM((2, 8, LANES), F32),
-            pltpu.VMEM((2, 8, LANES), F32),
+            pltpu.VMEM((4, 8, LANES), F32),
+            pltpu.VMEM((4, 8, LANES), F32),
             pltpu.VMEM((CHUNKS, 8, LANES), F32),
             pltpu.VMEM((CHUNKS, 8, LANES), F32),
             pltpu.VMEM((CHUNKS, 8, LANES), F32),
@@ -454,13 +509,13 @@
             pltpu.VMEM((PAIRS, GROUP, 2 * pair_rows, LANES), BF16),
             pltpu.VMEM((8, LANES), F32),
             pltpu.VMEM((8, LANES), F32),
-            dma((2,)),
+            dma((3,)),
             dma((loads,)),
             dma((loads,)),
-            dma((2,)),
-            dma((2,)),
-            dma((2, CHUNKS)),
-            dma((2, CHUNKS)),
+            dma((4,)),
+            dma((4,)),
+            dma((2, CHUNKS + AHEAD)),
+            dma((2, CHUNKS + AHEAD)),
             dma((CHUNKS,)),
             dma((CHUNKS,)),
             dma((CHUNKS, GROUP - 1)),
@@ -473,8 +528,8 @@
             dma((3,)),
             dma((3,)),
             dma((2,)),
-            dma((PAIRS,)),
-            dma((PAIRS,)),
+            dma((PAIRS, GROUP)),
+            dma((PAIRS, GROUP)),
             dma((PAIRS, GROUP - 1)),
             dma((PAIRS, GROUP - 1)),
             dma((1,)),
@@ -483,22 +538,25 @@
         compiler_params=pltpu.CompilerParams(
             collective_id=0, has_side_effects=True, vmem_limit_bytes=MAIN_VMEM * MIB
         ),
-    )(teacher_hidden, student_hidden, sampled_ids.reshape(2, LANES), teacher_head, student_head)
-
-    step = 512
-    whole = lambda a: pl.BlockSpec(a.shape, lambda j: (0,) * a.ndim)
+    )(
+        *(
+            pltpu.with_memory_space_constraint(a, pltpu.HBM)
+            for a in (teacher_hidden, student_hidden, sampled_ids.reshape(2, LANES), teacher_head, student_head)
+        )
+    )
+
     head_grad, hid, kl, gap = pl.pallas_call(
         functools.partial(last_kernel, 1.0 / (toks * tokens)),
         name="head_grad",
-        grid=(pl.cdiv(width, step),),
         out_shape=(
             jax.ShapeDtypeStruct((feats, width), F32),
             jax.ShapeDtypeStruct(hid.shape, hid.dtype),
             jax.ShapeDtypeStruct(kl.shape, kl.dtype),
             jax.ShapeDtypeStruct(gap.shape, gap.dtype),
         ),
-        in_specs=[whole(ht), pl.BlockSpec((toks * tokens, step), lambda j: (0, j)), whole(hid), whole(kl), whole(gap)],
-        out_specs=(pl.BlockSpec((feats, step), lambda j: (0, j)), whole(hid), whole(kl), whole(gap)),
+        in_specs=[vmem] * 5,
+        out_specs=(anywhere, vmem, vmem, vmem),
+        scratch_shapes=[pltpu.VMEM((feats, width), F32), dma((len(tiles(width, STEP)),))],
         compiler_params=pltpu.CompilerParams(vmem_limit_bytes=LAST_VMEM * MIB),
     )(ht, g, hid, kl, gap)
     return (kl.reshape(tokens), gap.reshape(tokens), hid, head_grad)

time: 99.1 us -> 95.5 us (0.964)
  local copies, waits for them, and re-layouts: 3.21 us -> 0 us
    unnamed x6 -> x0, local copies, waits for them, and re-layouts: 3.21 us -> none
where the time goes in v3:
time: 95.5 us; the launch traced here: 95.4 us
  Pallas kernels  94.5 us (99%)
    pallas_call x1, Pallas kernels, body(): pl.pallas_call(main_kernel, name='exchange', out_shape=(jax.ShapeDtypeStr...  90.1 us
    pallas_call x1, Pallas kernels, body(): pl.pallas_call(functools.partial(last_kernel, 1.0 / (toks * tokens)), nam...  4.44 us

profile of v3, /device:TPU:1, one launch (start us, length us, event | category | flops | bytes accessed | tf_op | source)
XLA Modules:
  0.0 95.4 jit_solution(6112321360127171393)
XLA Ops:
  0.6 90.1 %exchange.1 = (bf16[1024,2432]{1,0:T(8,128)(2,1)S(1)}, bf16[512,1024]{1,0:T(8,128)(2,1)S(1)}, bf16[256,128]{1,0:T(8,128)(2,1)S(1)}, f32[2,128]{1,0:T(2,128)S(1)}, f32[2,128]{1,0:T(2,128)S(1)}) custom-call(bf16[256,2560]{1,0:T(8,128)(2,1)} %th_in.1, bf16[256,2048]{1,0:T(8,128)(2,1)} %sh_in.1, s32[2,128]{1,0:T(2,128)} %bitcast.3, bf16[2560,2432]{1,0:T(8,128)(2,1)} %thead.1, ...), custom_call_target="tpu_custom_call" | custom-call | tf_op jit(solution)/shard_map/exchange/pallas_call | solution.py:473
  90.7 4.4 %head_grad.1 = (f32[512,2432]{1,0:T(8,128)}, bf16[256,128]{1,0:T(8,128)(2,1)}, f32[2,128]{1,0:T(2,128)}, f32[2,128]{1,0:T(2,128)}) custom-call(bf16[512,1024]{1,0:T(8,128)(2,1)S(1)} %get-tuple-element.13.ht, bf16[1024,2432]{1,0:T(8,128)(2,1)S(1)} %get-tuple-element.14.g, bf16[256,128]{1,0:T(8,128)(2,1)S(1)} %get-tuple-element.15.hid, ...), custom_call_target="tpu_custom_call" | custom-call | tf_op jit(solution)/shard_map/head_grad/pallas_call | solution.py:548

commit v4 on v3

--- a/solution.py
+++ b/solution.py
@@ -403,12 +403,9 @@
     for i in range(CHUNKS):
         end = i == CHUNKS - 1
         sums_and_stats(i)
-        if end:
-            join_core(i)
+        join_core(i)
         if i >= 1:
             grads(i - 1)
-        if not end:
-            join_core(i)
         if AHEAD < i + 2 < CHUNKS:
             partial_copy(0, i + 2).start()
         if i + 2 < CHUNKS:

time: 95.5 us -> 95.7 us (level)
  no operation moved by 1% of the time
where the time goes in v4:
time: 95.7 us; the launch traced here: 95.6 us
  Pallas kernels  94.8 us (99%)
    pallas_call x1, Pallas kernels, body(): pl.pallas_call(main_kernel, name='exchange', out_shape=(jax.ShapeDtypeStr...  90.4 us
    pallas_call x1, Pallas kernels, body(): pl.pallas_call(functools.partial(last_kernel, 1.0 / (toks * tokens)), nam...  4.44 us

profile of v4, /device:TPU:1, one launch (start us, length us, event | category | flops | bytes accessed | tf_op | source)
XLA Modules:
  0.0 95.6 jit_solution(13687866160461985806)
XLA Ops:
  0.6 90.4 %exchange.1 = (bf16[1024,2432]{1,0:T(8,128)(2,1)S(1)}, bf16[512,1024]{1,0:T(8,128)(2,1)S(1)}, bf16[256,128]{1,0:T(8,128)(2,1)S(1)}, f32[2,128]{1,0:T(2,128)S(1)}, f32[2,128]{1,0:T(2,128)S(1)}) custom-call(bf16[256,2560]{1,0:T(8,128)(2,1)} %th_in.1, bf16[256,2048]{1,0:T(8,128)(2,1)} %sh_in.1, s32[2,128]{1,0:T(2,128)} %bitcast.3, bf16[2560,2432]{1,0:T(8,128)(2,1)} %thead.1, ...), custom_call_target="tpu_custom_call" | custom-call | tf_op jit(solution)/shard_map/exchange/pallas_call | solution.py:470
  91.0 4.4 %head_grad.1 = (f32[512,2432]{1,0:T(8,128)}, bf16[256,128]{1,0:T(8,128)(2,1)}, f32[2,128]{1,0:T(2,128)}, f32[2,128]{1,0:T(2,128)}) custom-call(bf16[512,1024]{1,0:T(8,128)(2,1)S(1)} %get-tuple-element.13.ht, bf16[1024,2432]{1,0:T(8,128)(2,1)S(1)} %get-tuple-element.14.g, bf16[256,128]{1,0:T(8,128)(2,1)S(1)} %get-tuple-element.15.hid, ...), custom_call_target="tpu_custom_call" | custom-call | tf_op jit(solution)/shard_map/head_grad/pallas_call | solution.py:545
